TPU v7x, 32 devices: a whole 2x2x4 slice. The times are simulated.
32 devices in a mesh: dp: 8 (over z, x), tensor: 4 (over y, core).
Axes of the slice: x: 2, y: 2, z: 4, core: 2. Of those that a mesh axis runs over, the one named last changes fastest.
Arguments:
- tokens_in: bfloat16 [12288, 768], P('dp'), may hold values from -6 to 6
- cotangent: bfloat16 [12288, 768], P('dp'), may hold values from -6 to 6
- span_mask: int32 [12288], P('dp'), may hold values from 0 to 1, as said below
- lengths: int32 [24], P('dp'), may hold values from 128 to 512, as said below
- step: int32 [1], replicated, may hold values from 1000 to 31999
- warmup: int32 [1], replicated, may hold values from 1000 to 29999
- total: int32 [1], replicated, may hold values from 32000 to 40000
- w_qkv: float32 [768, 3, 768], P(None, None, 'tensor'), may hold values from -0.21875 to 0.21875
- w_out: float32 [768, 768], P(None, 'tensor'), may hold values from -1.25 to 1.25
- w_in: float32 [768, 3072], P(None, 'tensor'), may hold values from -0.21875 to 0.21875
- w_back: float32 [768, 3072], P(None, 'tensor'), may hold values from -0.109375 to 0.109375
- gains: float32 [2, 768], replicated, may hold values from 0.5 to 1.5
- biases: float32 [6, 768], replicated, may hold values from -3 to 3
- bias_in: float32 [3072], replicated, may hold values from -3 to 3
- mom_qkv: float32 [2, 768, 3, 768], P(None, 'dp', None, 'tensor'), as said below
- mom_out: float32 [2, 768, 768], P(None, 'dp', 'tensor'), as said below
- mom_in: float32 [2, 768, 3072], P(None, 'dp', 'tensor'), as said below
- mom_back: float32 [2, 768, 3072], P(None, 'dp', 'tensor'), as said below
- mom_gains: float32 [2, 2, 768], replicated, as said below
- mom_biases: float32 [2, 6, 768], replicated, as said below
- mom_bias_in: float32 [2, 3072], replicated, as said below
Outputs:
- normed_out: bfloat16 [12288, 768], P('dp')
- input_grad: float32 [12288, 768], P('dp')
- change_qkv: float32 [768, 3, 768], P(None, None, 'tensor')
- change_out_proj: float32 [768, 768], P(None, 'tensor')
- change_in_proj: float32 [768, 3072], P(None, 'tensor')
- change_back_proj: float32 [768, 3072], P(None, 'tensor')
- change_gains: float32 [2, 768], replicated
- change_biases: float32 [6, 768], replicated
- change_bias_in: float32 [3072], replicated
- new_mom_qkv: float32 [2, 768, 3, 768], P(None, 'dp', None, 'tensor')
- new_mom_out: float32 [2, 768, 768], P(None, 'dp', 'tensor')
- new_mom_in: float32 [2, 768, 3072], P(None, 'dp', 'tensor')
- new_mom_back: float32 [2, 768, 3072], P(None, 'dp', 'tensor')
- new_mom_gains: float32 [2, 2, 768], replicated
- new_mom_biases: float32 [2, 6, 768], replicated
- new_mom_bias_in: float32 [2, 3072], replicated
Inputs may be any that keep to these rules, and one draw needn't show every extreme that they name: `span_mask`: marked positions lie below their sequence's length and form unions of spans of 1 to 10 positions; each sequence has at most 76 of them, and in every draw each of the 3 sequences of some index of dp has exactly 76. `lengths`: a sequence's real tokens stand at its start, the rest is padding. step < total. warmup < total. `mom_qkv`: index 1 of the leading dimension holds positive second moments. `mom_out`: index 1 of the leading dimension holds positive second moments. `mom_in`: index 1 of the leading dimension holds positive second moments. `mom_back`: index 1 of the leading dimension holds positive second moments. `mom_gains`: index 1 of the leading dimension holds positive second moments. `mom_biases`: index 1 of the leading dimension holds positive second moments. `mom_bias_in`: index 1 of the leading dimension holds positive second moments.
All inputs are finite; a program needn't handle non-finite values.
Results may differ from a plain program's by a relative error of at most 0.017.
The roundings to bfloat16 on the way count: a program that leaves them out, or rounds other values in their place, can miss the bound.
Values sent between devices are 32-bit elements; how exact they have to be, the bound alone decides.
A program may use at most 128 MiB of HBM per device.

v0:
```python
import math
import jax
import jax.numpy as jnp
from jax import lax
from jax.sharding import PartitionSpec as P

HD = 64
NORM_EPS = 1e-12
BETA_ONE = 0.9
BETA_TWO = 0.999
ADAM_EPS = 1e-06
WEIGHT_DECAY = 0.01


def layer_norm(values, gain, shift):
    center = values - jnp.mean(values, axis=-1, keepdims=True)
    spread = jnp.mean(center * center, axis=-1, keepdims=True)
    return center * lax.rsqrt(spread + NORM_EPS) * gain + shift


def exact_gelu(values):
    return jax.nn.gelu(values, approximate=False)


def outer_sum(left, right):
    return jnp.einsum("ta,tb->ab", left, right, preferred_element_type=jnp.float32)


def adam_step(weight, grad, moments, ratio, corr_one, corr_two, decay):
    first = BETA_ONE * moments[0] + (1.0 - BETA_ONE) * grad
    second = BETA_TWO * moments[1] + (1.0 - BETA_TWO) * grad * grad
    update = first / corr_one / (jnp.sqrt(second / corr_two) + ADAM_EPS) + decay * weight
    return (-ratio * update, jnp.stack([first, second]))


def on_device(
    tokens_in,
    cotangent,
    span_mask,
    lengths,
    step,
    warmup,
    total,
    w_qkv,
    w_out,
    w_in,
    w_back,
    gains,
    biases,
    bias_in,
    mom_qkv,
    mom_out,
    mom_in,
    mom_back,
    mom_gains,
    mom_biases,
    mom_bias_in,
):
    row_count, model_width = tokens_in.shape
    seq_count = lengths.shape[0]
    seq_length = row_count // seq_count
    head_cols = w_qkv.shape[2]
    hidden_cols = w_in.shape[1]
    head_size = HD
    local_heads = head_cols // head_size
    query_scale = 1.0 / math.sqrt(head_size)
    tensor_slot = lax.axis_index("tensor")
    bias_query = lax.dynamic_slice_in_dim(biases[0], tensor_slot * head_cols, head_cols)
    bias_value = lax.dynamic_slice_in_dim(biases[1], tensor_slot * head_cols, head_cols)
    bias_hidden = lax.dynamic_slice_in_dim(bias_in, tensor_slot * hidden_cols, hidden_cols)
    qkv_low = w_qkv.astype(jnp.bfloat16).reshape(model_width, 3 * head_cols)
    out_low = w_out.astype(jnp.bfloat16)
    in_low = w_in.astype(jnp.bfloat16)
    down_low = w_back.astype(jnp.bfloat16)
    projected = jnp.dot(tokens_in, qkv_low, preferred_element_type=jnp.float32).reshape(
        row_count, 3, head_cols
    )
    attn_shape = (seq_count, seq_length, local_heads, head_size)
    queries = (
        ((projected[:, 0] + bias_query) * query_scale).astype(jnp.bfloat16).reshape(attn_shape)
    )
    keys = projected[:, 1].astype(jnp.bfloat16).reshape(attn_shape)
    values = (projected[:, 2] + bias_value).astype(jnp.bfloat16).reshape(attn_shape)
    positions = jnp.arange(seq_length, dtype=jnp.int32)
    inside = positions[None, :] < lengths[:, None]
    key_bias = jnp.where(inside, 0.0, -1000000000.0).astype(jnp.float32)

    def score_block():
        raw = jnp.einsum("sqhd,skhd->shqk", queries, keys, preferred_element_type=jnp.float32)
        return raw + key_bias[:, None, None, :]

    scores = score_block()
    peak = jnp.max(scores, axis=-1, keepdims=True)
    log_total = peak + jnp.log(jnp.sum(jnp.exp(scores - peak), axis=-1, keepdims=True))
    probs_low = jnp.exp(scores - log_total).astype(jnp.bfloat16)
    context_low = (
        jnp.einsum("shqk,skhd->sqhd", probs_low, values, preferred_element_type=jnp.float32)
        .reshape(row_count, head_cols)
        .astype(jnp.bfloat16)
    )
    attn_part = jnp.einsum("tc,dc->td", context_low, out_low, preferred_element_type=jnp.float32)
    attn_sum = lax.psum(attn_part, "tensor")
    residual_one = tokens_in.astype(jnp.float32) + attn_sum + biases[2]
    normed = layer_norm(residual_one, gains[0], biases[3])
    normed_low = normed.astype(jnp.bfloat16)
    pre_act = jnp.dot(normed_low, in_low, preferred_element_type=jnp.float32) + bias_hidden
    act_low = exact_gelu(pre_act).astype(jnp.bfloat16)
    down_part = jnp.einsum("tf,df->td", act_low, down_low, preferred_element_type=jnp.float32)
    down_sum = lax.psum(down_part, "tensor")
    residual_two = normed + down_sum + biases[4]
    result, norm_two_back = jax.vjp(layer_norm, residual_two, gains[1], biases[5])
    normed_out = result.astype(jnp.bfloat16)
    live_int = inside.reshape(row_count).astype(jnp.int32) * span_mask
    live = live_int.astype(jnp.float32)
    grad_result = cotangent.astype(jnp.float32) * live[:, None]
    d_res_two, d_gain_two, d_shift_two = norm_two_back(grad_result)
    d_res_two_low = d_res_two.astype(jnp.bfloat16)
    grad_back = outer_sum(d_res_two_low, act_low)
    d_act = jnp.dot(d_res_two_low, down_low, preferred_element_type=jnp.float32)
    _, gelu_back = jax.vjp(exact_gelu, pre_act)
    d_pre = gelu_back(d_act)[0]
    d_pre_low = d_pre.astype(jnp.bfloat16)
    grad_in = outer_sum(normed_low, d_pre_low)
    d_normed_part = jnp.einsum("tf,df->td", d_pre_low, in_low, preferred_element_type=jnp.float32)
    d_normed = lax.psum(d_normed_part, "tensor") + d_res_two
    _, norm_one_back = jax.vjp(layer_norm, residual_one, gains[0], biases[3])
    d_res_one, d_gain_one, d_shift_one = norm_one_back(d_normed)
    d_res_one_low = d_res_one.astype(jnp.bfloat16)
    grad_out_proj = outer_sum(d_res_one_low, context_low)
    d_context = (
        jnp.dot(d_res_one_low, out_low, preferred_element_type=jnp.float32)
        .astype(jnp.bfloat16)
        .reshape(attn_shape)
    )
    probs = jnp.exp(score_block() - log_total)
    probs_again = probs.astype(jnp.bfloat16)
    d_probs = jnp.einsum("sqhd,skhd->shqk", d_context, values, preferred_element_type=jnp.float32)
    d_values = jnp.einsum(
        "shqk,sqhd->skhd", probs_again, d_context, preferred_element_type=jnp.float32
    ).reshape(row_count, head_cols)
    d_scores = (probs * (d_probs - jnp.sum(probs * d_probs, axis=-1, keepdims=True))).astype(
        jnp.bfloat16
    )
    d_queries = (
        jnp.einsum("shqk,skhd->sqhd", d_scores, keys, preferred_element_type=jnp.float32).reshape(
            row_count, head_cols
        )
        * query_scale
    )
    d_keys = jnp.einsum(
        "shqk,sqhd->skhd", d_scores, queries, preferred_element_type=jnp.float32
    ).reshape(row_count, head_cols)
    d_proj_low = (
        jnp.stack([d_queries, d_keys, d_values], axis=1)
        .astype(jnp.bfloat16)
        .reshape(row_count, 3 * head_cols)
    )
    grad_qkv = outer_sum(tokens_in, d_proj_low).reshape(model_width, 3, head_cols)
    d_entry_part = jnp.einsum("tc,dc->td", d_proj_low, qkv_low, preferred_element_type=jnp.float32)
    input_grad = lax.psum(d_entry_part, "tensor") + d_res_one
    first_rank = (tensor_slot == 0).astype(jnp.float32)
    width_zero = jnp.zeros((model_width,), jnp.float32)

    def place_heads(partial_sum):
        return lax.dynamic_update_slice_in_dim(width_zero, partial_sum, tensor_slot * head_cols, 0)

    grad_gains = jnp.stack([d_gain_one, d_gain_two]) * first_rank
    grad_biases = jnp.stack(
        [
            place_heads(jnp.sum(d_queries, axis=0)),
            place_heads(jnp.sum(d_values, axis=0)),
            jnp.sum(d_res_one, axis=0) * first_rank,
            d_shift_one * first_rank,
            jnp.sum(d_res_two, axis=0) * first_rank,
            d_shift_two * first_rank,
        ]
    )
    grad_bias_in = lax.dynamic_update_slice_in_dim(
        jnp.zeros(bias_in.shape, jnp.float32), jnp.sum(d_pre, axis=0), tensor_slot * hidden_cols, 0
    )
    grad_gains, grad_biases, grad_bias_in = lax.psum(
        (grad_gains, grad_biases, grad_bias_in), ("dp", "tensor")
    )
    data_slot = lax.axis_index("dp")
    shard_rows = model_width // lax.axis_size("dp")
    summed = lax.psum((grad_qkv, grad_out_proj, grad_in, grad_back), "dp")
    owned = tuple(
        (
            lax.dynamic_slice_in_dim(whole_sum, data_slot * shard_rows, shard_rows, 0)
            for whole_sum in summed
        )
    )
    clock = step[0].astype(jnp.float32)
    warm = warmup[0].astype(jnp.float32)
    horizon = total[0].astype(jnp.float32)
    ratio = jnp.minimum(clock / warm, (horizon - clock) / (horizon - warm))
    corr_one = 1.0 - jnp.power(BETA_ONE, clock)
    corr_two = 1.0 - jnp.power(BETA_TWO, clock)
    change_rows = []
    fresh_moments = []
    for weight, grad_rows, moment in zip(
        (w_qkv, w_out, w_in, w_back), owned, (mom_qkv, mom_out, mom_in, mom_back)
    ):
        weight_rows = lax.dynamic_slice_in_dim(weight, data_slot * shard_rows, shard_rows, 0)
        row_change, new_moment = adam_step(
            weight_rows, grad_rows, moment, ratio, corr_one, corr_two, WEIGHT_DECAY
        )
        change_rows.append(row_change)
        fresh_moments.append(new_moment)
    change_qkv, change_out_proj, change_in_proj, change_back_proj = (
        lax.all_gather(change_rows[0], "dp", axis=0, tiled=True),
        lax.all_gather(change_rows[1], "dp", axis=0, tiled=True),
        lax.all_gather(change_rows[2], "dp", axis=0, tiled=True),
        lax.all_gather(change_rows[3], "dp", axis=0, tiled=True),
    )
    change_gains, new_mom_gains = adam_step(
        gains, grad_gains, mom_gains, ratio, corr_one, corr_two, 0.0
    )
    change_biases, new_mom_biases = adam_step(
        biases, grad_biases, mom_biases, ratio, corr_one, corr_two, 0.0
    )
    change_bias_in, new_mom_bias_in = adam_step(
        bias_in, grad_bias_in, mom_bias_in, ratio, corr_one, corr_two, 0.0
    )
    return (
        normed_out,
        input_grad,
        change_qkv,
        change_out_proj,
        change_in_proj,
        change_back_proj,
        change_gains,
        change_biases,
        change_bias_in,
        fresh_moments[0],
        fresh_moments[1],
        fresh_moments[2],
        fresh_moments[3],
        new_mom_gains,
        new_mom_biases,
        new_mom_bias_in,
    )


def solution(mesh):
    in_specs = (
        P("dp", None),
        P("dp", None),
        P("dp"),
        P("dp"),
        P(),
        P(),
        P(),
        P(None, None, "tensor"),
        P(None, "tensor"),
        P(None, "tensor"),
        P(None, "tensor"),
        P(),
        P(),
        P(),
        P(None, "dp", None, "tensor"),
        P(None, "dp", "tensor"),
        P(None, "dp", "tensor"),
        P(None, "dp", "tensor"),
        P(),
        P(),
        P(),
    )
    out_specs = (
        P("dp", None),
        P("dp", None),
        P(None, None, "tensor"),
        P(None, "tensor"),
        P(None, "tensor"),
        P(None, "tensor"),
        P(),
        P(),
        P(),
        P(None, "dp", None, "tensor"),
        P(None, "dp", "tensor"),
        P(None, "dp", "tensor"),
        P(None, "dp", "tensor"),
        P(),
        P(),
        P(),
    )
    return jax.shard_map(
        on_device, mesh=mesh, in_specs=in_specs, out_specs=out_specs, check_vma=False
    )
```

profile of v0, /device:TPU:0, one launch (start us, length us, event | category | flops | bytes accessed | tf_op | source)
XLA Modules:
  0.0 939.9 jit_solution(9173336511828967916)
XLA Ops:
  7.2 3.8 fusion.10
  11.1 1.2 fusion.80
  12.6 1.1 convert_element_type.98
  13.8 0.9 squeeze.4
  14.7 1.9 squeeze.5
  16.6 2.9 add_reduce_fusion
  19.6 1.8 exponential_reduce_fusion
  21.8 1.4 copy-done
  23.2 1.7 fusion.12
  25.6 3.0 fusion.45
  28.9 0.8 dynamic_slice.35
  29.7 95.8 %all-reduce.8.cloned.1.call-done = f32[1536,768]{1,0:T(8,128)} async-done(((f32[1536,768]{1,0:T(8,128)}), f32[1536,768]{1,0:T(8,128)}) %all-reduce.8.cloned.1.call-update) | async-done | bytes 4718608 | tf_op jit(solution)/shard_map/psum | solution.py:102
  125.6 3.8 fusion.79
  129.4 0.7 multiply_reduce_fusion.6
  130.1 2.6 copy-done.19
  132.8 14.4 %multiply_convert_fusion.1 = (bf16[1536,768]{1,0:T(8,128)(2,1)S(1)}, f32[1536,768]{1,0:T(8,128)}, f32[1536,768]{1,0:T(8,128)}) fusion(f32[768]{0:T(1024)S(1)} %dynamic_slice.35, f32[768,768]{1,0:T(8,128)S(1)} %copy-done.19, f32[1536,768]{1,0:T(8,128)S(1)} %get-tuple-element.96, f32[768]{0:T(1024)S(1)} %get-tuple-element.125, ...), kind=kOutput, calls=%fused_computation.21 | convolution fusion | flops 1896284160 | bytes 18895872 | tf_op jit(solution)/shard_map/dot_general | solution.py:106
  147.1 1.4 copy-done.39
  148.5 4.3 fusion.24
  153.6 93.7 %all-reduce.10.cloned.1.call-done = f32[1536,768]{1,0:T(8,128)} async-done(((f32[1536,768]{1,0:T(8,128)}), f32[1536,768]{1,0:T(8,128)}) %all-reduce.10.cloned.1.call-update) | async-done | bytes 4718608 | tf_op jit(solution)/shard_map/psum | solution.py:109
  247.2 4.7 fusion.77
  252.6 1.0 copy-done.4
  253.6 2.8 multiply_reduce_fusion.1
  256.5 3.7 fusion.76
  260.2 4.5 fusion.85
  264.7 1.4 copy-done.40
  266.1 4.3 fusion.17
  270.5 6.9 fusion.72
  277.4 6.4 fusion.15
  283.8 81.0 %all-reduce.12.cloned.1.call-done = f32[1536,768]{1,0:T(8,128)} async-done(((f32[1536,768]{1,0:T(8,128)}), f32[1536,768]{1,0:T(8,128)}) %all-reduce.12.cloned.1.call-update) | async-done | bytes 4718608 | tf_op jit(solution)/shard_map/psum | solution.py:125
  364.8 7.5 multiply_reduce_fusion.2
  372.2 3.8 fusion.75
  376.1 2.4 fusion.73
  378.5 1.0 convolution_convert_fusion
  380.0 6.4 fusion.84
  386.4 5.7 multiply_reduce_fusion
  392.2 2.3 multiply_convert_fusion
  394.5 1.6 convolution_bitcast_fusion.2
  396.1 1.6 fusion.83
  398.2 0.8 stack_reshape.7
  399.5 1.0 mul.594
  401.0 0.8 stack_reshape.6
  402.1 4.4 fusion.88
  406.5 2.9 copy.94
  409.5 5.7 convolution_bitcast_fusion
  417.9 1.2 constant_dynamic-slice_fusion.1
  419.3 247.8 %all-reduce.16.cloned.1.call-done = (f32[768,3,192]{2,0,1:T(8,128)}, f32[768,192]{1,0:T(8,128)}, f32[768,768]{1,0:T(8,128)}, f32[768,768]{1,0:T(8,128)}) async-done(((f32[768,3,192]{2,0,1:T(8,128)}, f32[768,192]{1,0:T(8,128)}, f32[768,768]{1,0:T(8,128)}, f32[768,768]{1,0:T(8,128)}), (f32[768,3,192]{2,0,1:T(8,128)}, f32[768,192]{1,0:T(8,128)}, f32[768,768]{1,0:T(8,128)}, ...) | async-done | bytes 7077904 | tf_op jit(solution)/shard_map/psum | solution.py:186
  667.1 1.9 fusion.50
  669.1 2.0 fusion.48
  671.2 2.2 fusion.49
  674.7 87.7 %all-reduce.14.cloned.1.call-done = f32[1536,768]{1,0:T(8,128)} async-done(((f32[1536,768]{1,0:T(8,128)}), f32[1536,768]{1,0:T(8,128)}) %all-reduce.14.cloned.1.call-update) | async-done | bytes 4718608 | tf_op jit(solution)/shard_map/psum | solution.py:160
  762.4 6.5 add_reduce_fusion.1
  769.0 41.3 %all-reduce = (f32[2,768]{1,0:T(2,128)S(1)}, f32[6,768]{1,0:T(8,128)S(1)}, f32[3072]{0:T(1024)S(1)}) all-reduce(f32[2,768]{1,0:T(2,128)S(1)} %maximum_multiply_fusion, f32[6,768]{1,0:T(8,128)S(1)} %stack.89, f32[3072]{0:T(1024)S(1)} %dynamic_update_slice.13), channel_id=1, replica_groups=mesh['dp'=8,'tensor'=4] {'dp','tensor'}, use_global_device_ids=true, to_apply=%region_21.22 | all-reduce | flops 9216 | bytes 73728 | tf_op jit(solution)/shard_map/psum | solution.py:181
  814.1 1.0 fusion.58
  815.1 33.2 %all_gather.13 = f32[768,192]{1,0:T(8,128)S(1)} all-gather(f32[96,192]{1,0:T(8,128)S(1)} %get-tuple-element.114), channel_id=1, replica_groups=mesh['dp'=8,'tensor'=4] {'dp'}, dimensions={0}, use_global_device_ids=true | all-gather | bytes 663552 | tf_op jit(solution)/shard_map/all_gather | solution.py:212
  848.3 1.1 copy.100
  849.4 0.7 pad_maximum_fusion.3
  850.1 0.9 pad_maximum_fusion
  850.9 0.9 pad_maximum_fusion.2
  851.8 0.9 pad_maximum_fusion.1
  852.6 2.9 copy.99
  855.5 19.2 %all-gather.6.cloned.1.call-done = f32[768,768]{1,0:T(8,128)} async-done(((f32[96,768]{1,0:T(8,128)}), f32[768,768]{1,0:T(8,128)}) %all-gather.6.cloned.1.call-update) | async-done | bytes 2359312 | tf_op jit(solution)/shard_map/all_gather | solution.py:213
  874.7 53.4 %all-gather.8.cloned.1.call-done = f32[768,768]{1,0:T(8,128)} async-done(((f32[96,768]{1,0:T(8,128)}), f32[768,768]{1,0:T(8,128)}) %all-gather.8.cloned.1.call-update) | async-done | bytes 2359312 | tf_op jit(solution)/shard_map/all_gather | solution.py:214
  928.1 3.4 copy.176
  931.5 1.4 copy.177
  (173 shorter events, 10.9 us)
Async XLA Ops:
  7.2 118.4 %all-reduce.8.cloned.1.call-start = ((), (), s32[]{:S(2)}) async-start(), calls=%async_computation | async-start | bytes 9437184 | tf_op jit(solution)/shard_map/psum | solution.py:102
  11.0 1.3 copy-start.38
  11.0 1.3 copy-start.15
  12.6 6.9 copy-start.17
  19.6 3.6 copy-start
  21.4 3.5 copy-start.10
  23.2 1.8 copy-start.5
  23.2 2.4 copy-start.8
  28.7 1.0 copy-start.25
  28.7 218.5 %all-reduce.10.cloned.1.call-start = ((), (), s32[]{:S(2)}) async-start(), calls=%async_computation.1 | async-start | bytes 9437184 | tf_op jit(solution)/shard_map/psum | solution.py:109
  129.4 17.8 %copy-start.1 = (f32[1536,768]{1,0:T(8,128)}, f32[1536,768]{1,0:T(8,128)S(1)}, u32[]{:S(2)}) copy-start(f32[1536,768]{1,0:T(8,128)S(1)} %get-tuple-element.96) | copy-start | bytes 14155780
  129.4 3.4 copy-start.19
  132.8 15.8 %copy-start.21 = (f32[768,768]{1,0:T(8,128)S(1)}, f32[768,768]{1,0:T(8,128)}, u32[]{:S(2)}) copy-start(f32[768,768]{1,0:T(8,128)} %param.31) | copy-start | bytes 7077892
  147.1 1.4 copy-start.39
  152.9 0.7 copy-start.36
  152.9 211.9 %all-reduce.12.cloned.1.call-start = ((), (), s32[]{:S(2)}) async-start(), calls=%async_computation.2 | async-start | bytes 9437184 | tf_op jit(solution)/shard_map/psum | solution.py:125
  252.0 1.7 copy-start.4
  253.6 6.5 slice-start.3
  253.6 6.5 slice-start.5
  256.5 3.7 copy-start.22
  256.5 3.7 slice-start.4
  256.5 3.7 slice-start.6
  260.2 4.6 copy-start.3
  260.2 5.9 copy-start.20
  264.7 1.4 copy-start.40
  270.4 396.7 %all-reduce.16.cloned.1.call-start = ((), (), s32[]{:S(2)}) async-start(), calls=%async_computation.7 | async-start | bytes 15728640 | tf_op jit(solution)/shard_map/psum | solution.py:186
  270.5 6.9 copy-start.41
  376.1 2.4 copy-start.2
  380.0 6.4 copy-start.6
  380.0 6.4 copy-start.11
  380.0 12.1 %slice-start = ((s8[9437184]{0:T(1024)(128)(4,1)}), s8[4194304]{0:T(1024)(128)(4,1)S(1)}, s32[]{:S(2)}) async-start(s8[9437184]{0:T(1024)(128)(4,1)} %bitcast.159), calls=%async_computation.8 | async-start | bytes 8388608
  380.0 12.1 %slice-start.1 = ((s8[9437184]{0:T(1024)(128)(4,1)}), s8[4194304]{0:T(1024)(128)(4,1)S(1)}, s32[]{:S(2)}) async-start(s8[9437184]{0:T(1024)(128)(4,1)} %bitcast.159), calls=%async_computation.9 | async-start | bytes 8388608
  386.4 5.7 slice-start.2
  392.1 2.3 copy-start.18
  394.5 1.6 copy-start.7
  409.5 352.9 %all-reduce.14.cloned.1.call-start = ((), (), s32[]{:S(2)}) async-start(), calls=%async_computation.3 | async-start | bytes 9437184 | tf_op jit(solution)/shard_map/psum | solution.py:160
  415.2 251.9 %copy-start.12 = (f32[2,96,3,192]{3,1,2,0:T(8,128)S(1)}, f32[2,96,3,192]{3,1,2,0:T(8,128)}, u32[]{:S(2)}) copy-start(f32[2,96,3,192]{3,1,2,0:T(8,128)} %param.35) | copy-start | bytes 1327108
  415.2 253.9 %copy-start.13 = (f32[2,96,768]{2,1,0:T(8,128)S(1)}, f32[2,96,768]{2,1,0:T(8,128)}, u32[]{:S(2)}) copy-start(f32[2,96,768]{2,1,0:T(8,128)} %param.37) | copy-start | bytes 1769476
  415.2 255.9 %copy-start.24 = (f32[2,3072]{1,0:T(2,128)S(1)}, f32[2,3072]{1,0:T(2,128)}, u32[]{:S(2)}) copy-start(f32[2,3072]{1,0:T(2,128)} %param.41) | copy-start | bytes 73732
  415.2 258.4 %copy-start.23 = (f32[2,6,768]{2,0,1:T(2,128)S(1)}, f32[2,6,768]{2,0,1:T(2,128)}, u32[]{:S(2)}) copy-start(f32[2,6,768]{2,0,1:T(2,128)} %param.40) | copy-start | bytes 110596
  415.3 258.4 %copy-start.28 = (f32[768]{0:T(1024)S(1)}, f32[768]{0:T(1024)}, u32[]{:S(2)}) copy-start(f32[768]{0:T(1024)} %get-tuple-element.66) | copy-start | bytes 9220
  415.3 258.4 %copy-start.29 = (f32[768]{0:T(1024)S(1)}, f32[768]{0:T(1024)}, u32[]{:S(2)}) copy-start(f32[768]{0:T(1024)} %get-tuple-element.69) | copy-start | bytes 9220
  415.3 258.4 %copy-start.37 = (f32[768]{0:T(1024)S(1)}, f32[768]{0:T(1024)}, u32[]{:S(2)}) copy-start(f32[768]{0:T(1024)} %get-tuple-element.140) | copy-start | bytes 9220
  415.3 258.7 %copy-start.30 = (f32[768]{0:T(1024)S(1)}, f32[768]{0:T(1024)}, u32[]{:S(2)}) copy-start(f32[768]{0:T(1024)} %get-tuple-element.64) | copy-start | bytes 9220
  415.3 258.7 %copy-start.32 = (f32[768]{0:T(1024)S(1)}, f32[768]{0:T(1024)}, u32[]{:S(2)}) copy-start(f32[768]{0:T(1024)} %get-tuple-element.68) | copy-start | bytes 9220
  415.3 258.8 %copy-start.31 = (f32[768]{0:T(1024)S(1)}, f32[768]{0:T(1024)}, u32[]{:S(2)}) copy-start(f32[768]{0:T(1024)} %get-tuple-element.98) | copy-start | bytes 9220
  415.3 258.8 %copy-start.34 = (f32[3,64]{1,0:T(4,128)S(1)}, f32[3,64]{1,0:T(4,128)}, u32[]{:S(2)}) copy-start(f32[3,64]{1,0:T(4,128)} %get-tuple-element.138) | copy-start | bytes 2308
  415.3 258.9 %copy-start.35 = (f32[3,64]{1,0:T(4,128)S(1)}, f32[3,64]{1,0:T(4,128)}, u32[]{:S(2)}) copy-start(f32[3,64]{1,0:T(4,128)} %get-tuple-element.136) | copy-start | bytes 2308
  415.3 437.3 %all-gather.4.cloned.1.call-start = ((), (), s32[]{:S(2)}) async-start(), calls=%async_computation.4 | async-start | bytes 2654208 | tf_op jit(solution)/shard_map/all_gather | solution.py:211
  669.0 205.7 %all-gather.6.cloned.1.call-start = ((), (), s32[]{:S(2)}) async-start(), calls=%async_computation.5 | async-start | bytes 2654208 | tf_op jit(solution)/shard_map/all_gather | solution.py:213
  671.1 257.0 %all-gather.8.cloned.1.call-start = ((), (), s32[]{:S(2)}) async-start(), calls=%async_computation.6 | async-start | bytes 2654208 | tf_op jit(solution)/shard_map/all_gather | solution.py:214
  674.6 135.7 %copy-start.16 = (f32[6,768]{1,0:T(8,128)S(1)}, f32[6,768]{1,0:T(8,128)}, u32[]{:S(2)}) copy-start(f32[6,768]{1,0:T(8,128)} %param.33) | copy-start | bytes 55300
  674.6 137.0 %copy-start.26 = (f32[2,768]{1,0:T(2,128)S(1)}, f32[2,768]{1,0:T(2,128)}, u32[]{:S(2)}) copy-start(f32[2,768]{1,0:T(2,128)} %param.32) | copy-start | bytes 18436
  674.6 137.0 %copy-start.33 = (f32[2,2,768]{2,1,0:T(2,128)S(1)}, f32[2,2,768]{2,1,0:T(2,128)}, u32[]{:S(2)}) copy-start(f32[2,2,768]{2,1,0:T(2,128)} %param.39) | copy-start | bytes 36868
  674.6 138.2 %copy-start.27 = (f32[3072]{0:T(1024)S(1)}, f32[3072]{0:T(1024)}, u32[]{:S(2)}) copy-start(f32[3072]{0:T(1024)} %param.34) | copy-start | bytes 36868
  674.6 139.5 %copy-start.14 = (f32[2,96,192]{2,1,0:T(8,128)S(1)}, f32[2,96,192]{2,1,0:T(8,128)}, u32[]{:S(2)}) copy-start(f32[2,96,192]{2,1,0:T(8,128)} %param.36) | copy-start | bytes 442372
  928.1 3.4 copy-start.9
Sparse Core Ops, SparseCore 0:
  28.8 96.7 all-reduce.7
  153.0 94.1 all-reduce.9
  270.5 94.1 all-reduce.11
  409.6 257.4 all-reduce.15
  669.3 93.0 all-reduce.13
  765.0 52.6 all-gather.3
  820.4 54.2 all-gather.5
  877.5 50.5 all-gather.7
where the time goes:
time: 948 us; the launch traced here: 940 us
  waiting for transfers between devices  679 us (72%)
  matrix products  80.9 us (9%)
  blocking collectives  74.5 us (8%)
  other arithmetic  52.6 us (6%)
  local copies, waits for them, and re-layouts  34.9 us (4%)
  between operations  17.7 us (2%)
    psum x1, waiting for transfers between devices, on_device(): summed = lax.psum((grad_qkv, grad_out_proj, grad_in, grad_back), 'dp')  248 us
    psum x1, waiting for transfers between devices, on_device(): attn_sum = lax.psum(attn_part, 'tensor')  95.8 us
    psum x1, waiting for transfers between devices, on_device(): down_sum = lax.psum(down_part, 'tensor')  93.7 us
    psum x1, waiting for transfers between devices, on_device(): input_grad = lax.psum(d_entry_part, 'tensor') + d_res_one  87.7 us
    psum x1, waiting for transfers between devices, on_device(): d_normed = lax.psum(d_normed_part, 'tensor') + d_res_two  81 us
    all_gather x1, waiting for transfers between devices, on_device(): lax.all_gather(change_rows[3], 'dp', axis=0, tiled=True)  53.4 us
    psum x1, blocking collectives, on_device(): lax.psum((grad_gains, grad_biases, grad_bias_in), ('dp', 'tensor'))  41.3 us
    all_gather x1, blocking collectives, on_device(): lax.all_gather(change_rows[1], 'dp', axis=0, tiled=True)  33.2 us
  transfers between devices with their start and end apart: 8, of which 7 were waited for; matrix products, arithmetic and copies ran while one was open for 5% of the time, Pallas kernels for 0%

commit v1 on v0

--- a/solution.py
+++ b/solution.py
@@ -99,7 +99,11 @@
         .astype(jnp.bfloat16)
     )
     attn_part = jnp.einsum("tc,dc->td", context_low, out_low, preferred_element_type=jnp.float32)
-    attn_sum = lax.psum(attn_part, "tensor")
+    attn_sum = attn_part
+    for hop in (1, 2):
+        attn_sum = attn_sum + lax.ppermute(
+            attn_sum, "tensor", [(dev, dev ^ hop) for dev in range(4)]
+        )
     residual_one = tokens_in.astype(jnp.float32) + attn_sum + biases[2]
     normed = layer_norm(residual_one, gains[0], biases[3])
     normed_low = normed.astype(jnp.bfloat16)

time: 948 us -> 970 us (1.023)
  local copies, waits for them, and re-layouts: 34.9 us -> 53.4 us
    ppermute x0 -> x2, waiting for transfers between devices: none -> 106 us  [on_device(): lax.ppermute(attn_sum, 'tensor', [(dev, dev ^ hop) for dev in range(4)])]
    psum x1 -> x0, waiting for transfers between devices: 95.8 us -> none  [on_device(): attn_sum = lax.psum(attn_part, 'tensor')]
    unnamed x106 -> x144, local copies, waits for them, and re-layouts: 18.4 us -> 33.6 us
  transfers between devices with their start and end apart: 8 -> 9, of which waited for: 7 -> 8; matrix products, arithmetic and copies ran while one was open for 5% -> 7% of each run, Pallas kernels for 0% -> 0%
where the time goes in v1:
time: 970 us; the launch traced here: 960 us
  waiting for transfers between devices  672 us (69%)
  matrix products  78.7 us (8%)
  blocking collectives  74.9 us (8%)
  other arithmetic  59.4 us (6%)
  local copies, waits for them, and re-layouts  53.4 us (6%)
  between operations  17.9 us (2%)
    psum x1, waiting for transfers between devices, on_device(): summed = lax.psum((grad_qkv, grad_out_proj, grad_in, grad_back), 'dp')  248 us
    ppermute x2, waiting for transfers between devices, on_device(): lax.ppermute(attn_sum, 'tensor', [(dev, dev ^ hop) for dev in range(4)])  106 us
    psum x1, waiting for transfers between devices, on_device(): down_sum = lax.psum(down_part, 'tensor')  89.8 us
    psum x1, waiting for transfers between devices, on_device(): d_normed = lax.psum(d_normed_part, 'tensor') + d_res_two  81.5 us
    psum x1, waiting for transfers between devices, on_device(): input_grad = lax.psum(d_entry_part, 'tensor') + d_res_one  80.6 us
    all_gather x1, waiting for transfers between devices, on_device(): lax.all_gather(change_rows[3], 'dp', axis=0, tiled=True)  53.3 us
    psum x1, blocking collectives, on_device(): lax.psum((grad_gains, grad_biases, grad_bias_in), ('dp', 'tensor'))  41.6 us
    unnamed x144, local copies, waits for them, and re-layouts  33.6 us
  transfers between devices with their start and end apart: 9, of which 8 were waited for; matrix products, arithmetic and copies ran while one was open for 7% of the time, Pallas kernels for 0%

profile of v1, /device:TPU:0, one launch (start us, length us, event | category | flops | bytes accessed | tf_op | source)
XLA Modules:
  0.0 959.6 jit_solution(16915727056688476704)
XLA Ops:
  7.2 3.8 fusion.10
  11.1 1.2 fusion.78
  13.2 1.2 convert_element_type.98
  14.4 0.9 squeeze.4
  15.3 1.9 squeeze.5
  17.2 3.5 add_reduce_fusion
  20.8 1.8 exponential_reduce_fusion
  22.9 1.5 copy-done
  24.5 1.7 fusion.12
  28.3 7.5 collective-permute-done
  35.8 3.2 add.278
  39.0 2.9 collective-permute-start.1
  41.8 2.8 copy.93
  46.1 98.2 %collective-permute-done.1 = f32[1536,768]{0,1:T(8,128)} collective-permute-done((f32[1536,768]{0,1:T(8,128)}, f32[1536,768]{0,1:T(8,128)}, u32[]{:S(2)}, u32[]{:S(2)}) %collective-permute-start.1) | collective-permute-done | bytes 4718624 | tf_op jit(solution)/shard_map/ppermute | solution.py:104
  144.3 4.6 fusion.77
  150.1 2.2 copy-done.32
  152.3 14.8 %multiply_convert_fusion.1 = (bf16[1536,768]{1,0:T(8,128)(2,1)S(1)}, f32[1536,768]{1,0:T(8,128)}, f32[1536,768]{1,0:T(8,128)}) fusion(f32[768]{0:T(1024)S(1)} %dynamic_slice.35, f32[768,768]{1,0:T(8,128)S(1)} %copy-done.32, f32[1536,768]{0,1:T(8,128)S(1)} %get-tuple-element.96, f32[768]{0:T(1024)S(1)} %copy-done.42, f32[768]{0:T(1024)S(1)} %get-tuple-element.75, ...), kind=kOutput, calls=%fused_computation.21 | convolution fusion | flops 1896284160 | bytes 18895872 | tf_op jit(solution)/shard_map/dot_general | solution.py:110
  167.1 1.4 copy-done.56
  168.5 4.2 fusion.26
  174.1 3.2 copy.100
  177.3 1.3 select_convert_fusion
  178.6 89.8 %all-reduce.7.cloned.1.call-done = f32[1536,768]{0,1:T(8,128)} async-done(((f32[1536,768]{0,1:T(8,128)}), f32[1536,768]{0,1:T(8,128)}) %all-reduce.7.cloned.1.call-update) | async-done | bytes 4718608 | tf_op jit(solution)/shard_map/psum | solution.py:113
  268.4 4.5 fusion.75
  273.7 2.9 multiply_reduce_fusion.1
  276.6 3.7 fusion.74
  280.4 4.7 fusion.83
  285.0 1.4 copy-done.57
  286.5 4.2 fusion.17
  290.8 6.7 fusion.19
  297.5 6.0 fusion.15
  303.5 81.5 %all-reduce.9.cloned.1.call-done = f32[1536,768]{0,1:T(8,128)} async-done(((f32[1536,768]{0,1:T(8,128)}), f32[1536,768]{0,1:T(8,128)}) %all-reduce.9.cloned.1.call-update) | async-done | bytes 4718608 | tf_op jit(solution)/shard_map/psum | solution.py:129
  385.0 7.4 multiply_reduce_fusion.2
  392.4 3.6 fusion.73
  396.0 2.3 fusion.21
  399.6 6.4 fusion.82
  406.0 5.7 multiply_reduce_fusion
  411.7 2.4 multiply_convert_fusion
  414.1 1.6 convolution_bitcast_fusion.2
  415.7 1.6 fusion.81
  419.2 1.0 mul.594
  421.8 4.4 fusion.86
  426.2 2.9 copy.113
  429.2 5.7 convolution_bitcast_fusion
  437.4 1.2 constant_dynamic-slice_fusion.1
  438.8 248.0 %all-reduce.13.cloned.1.call-done = (f32[768,3,192]{2,0,1:T(8,128)}, f32[768,192]{1,0:T(8,128)}, f32[768,768]{1,0:T(8,128)}, f32[768,768]{1,0:T(8,128)}) async-done(((f32[768,3,192]{2,0,1:T(8,128)}, f32[768,192]{1,0:T(8,128)}, f32[768,768]{1,0:T(8,128)}, f32[768,768]{1,0:T(8,128)}), (f32[768,3,192]{2,0,1:T(8,128)}, f32[768,192]{1,0:T(8,128)}, f32[768,768]{1,0:T(8,128)}, ...) | async-done | bytes 7077904 | tf_op jit(solution)/shard_map/psum | solution.py:190
  686.8 2.2 fusion.50
  689.0 2.3 fusion.48
  691.4 1.5 slice_multiply_fusion.1
  692.8 2.6 fusion.49
  696.2 1.0 copy.132
  697.2 0.9 fusion.79
  698.2 2.4 copy.118
  701.4 80.6 %all-reduce.11.cloned.1.call-done = f32[1536,768]{0,1:T(8,128)} async-done(((f32[1536,768]{0,1:T(8,128)}), f32[1536,768]{0,1:T(8,128)}) %all-reduce.11.cloned.1.call-update) | async-done | bytes 4718608 | tf_op jit(solution)/shard_map/psum | solution.py:164
  782.1 6.5 add_reduce_fusion.1
  788.6 41.6 %all-reduce = (f32[2,768]{1,0:T(2,128)S(1)}, f32[6,768]{1,0:T(8,128)S(1)}, f32[3072]{0:T(1024)S(1)}) all-reduce(f32[2,768]{1,0:T(2,128)S(1)} %maximum_multiply_fusion, f32[6,768]{1,0:T(8,128)S(1)} %stack.89, f32[3072]{0:T(1024)S(1)} %dynamic_update_slice.13), channel_id=1, replica_groups=mesh['dp'=8,'tensor'=4] {'dp','tensor'}, use_global_device_ids=true, to_apply=%region_20.21 | all-reduce | flops 9216 | bytes 73728 | tf_op jit(solution)/shard_map/psum | solution.py:185
  831.6 6.1 copy.119
  840.2 1.0 fusion.58
  841.2 33.3 %all_gather.13 = f32[768,192]{1,0:T(8,128)S(1)} all-gather(f32[96,192]{1,0:T(8,128)S(1)} %get-tuple-element.114), channel_id=1, replica_groups=mesh['dp'=8,'tensor'=4] {'dp'}, dimensions={0}, use_global_device_ids=true | all-gather | bytes 663552 | tf_op jit(solution)/shard_map/all_gather | solution.py:216
  874.5 1.1 copy.121
  878.9 2.9 copy.120
  881.8 12.5 %all-gather.6.cloned.1.call-done = f32[768,768]{1,0:T(8,128)} async-done(((f32[96,768]{1,0:T(8,128)}), f32[768,768]{1,0:T(8,128)}) %all-gather.6.cloned.1.call-update) | async-done | bytes 2359312 | tf_op jit(solution)/shard_map/all_gather | solution.py:217
  894.3 53.3 %all-gather.8.cloned.1.call-done = f32[768,768]{1,0:T(8,128)} async-done(((f32[96,768]{1,0:T(8,128)}), f32[768,768]{1,0:T(8,128)}) %all-gather.8.cloned.1.call-update) | async-done | bytes 2359312 | tf_op jit(solution)/shard_map/all_gather | solution.py:218
  947.6 3.4 copy.200
  951.0 1.4 copy.201
  (213 shorter events, 21.9 us)
Async XLA Ops:
  7.2 261.2 %all-reduce.7.cloned.1.call-start = ((), (), s32[]{:S(2)}) async-start(), calls=%async_computation | async-start | bytes 9437184 | tf_op jit(solution)/shard_map/psum | solution.py:113
  13.2 7.5 copy-start.23
  17.2 3.5 copy-start.4
  20.8 3.7 copy-start
  22.6 3.6 copy-start.16
  24.4 2.5 copy-start.10
  27.7 8.1 collective-permute-start
  39.0 6.5 copy-start.37
  39.0 105.3 %collective-permute-start.1 = (f32[1536,768]{0,1:T(8,128)}, f32[1536,768]{0,1:T(8,128)}, u32[]{:S(2)}, u32[]{:S(2)}) collective-permute-start(f32[1536,768]{0,1:T(8,128)} %add.278), channel_id=1, source_target_pairs={{0,2},{1,3},{2,0},{3,1},{4,6},{5,7},{6,4},{7,5},{8,10},{9,11},{10,... | collective-permute-start | bytes 14155784 | tf_op jit(solution)/shard_map/ppermute | solution.py:104
  45.5 104.6 %copy-start.52 = (f32[768]{0:T(1024)}, f32[768]{0:T(1024)S(1)}, u32[]{:S(2)}) copy-start(f32[768]{0:T(1024)S(1)} %dynamic_slice.35) | copy-start | bytes 9220
  46.1 104.0 %copy-start.28 = (f32[768]{0:T(1024)}, f32[768]{0:T(1024)S(1)}, u32[]{:S(2)}) copy-start(f32[768]{0:T(1024)S(1)} %get-tuple-element.75) | copy-start | bytes 9220
  148.9 18.2 %copy-start.1 = (f32[1536,768]{0,1:T(8,128)}, f32[1536,768]{0,1:T(8,128)S(1)}, u32[]{:S(2)}) copy-start(f32[1536,768]{0,1:T(8,128)S(1)} %get-tuple-element.96) | copy-start | bytes 14155780
  148.9 3.4 copy-start.32
  148.9 3.4 copy-start.42
  150.0 17.0 %copy-start.19 = (f32[1536]{0:T(1024)}, f32[1536]{0:T(1024)S(1)}, u32[]{:S(2)}) copy-start(f32[1536]{0:T(1024)S(1)} %fusion.63) | copy-start | bytes 18436
  152.3 16.2 %copy-start.34 = (f32[768,768]{1,0:T(8,128)S(1)}, f32[768,768]{1,0:T(8,128)}, u32[]{:S(2)}) copy-start(f32[768,768]{1,0:T(8,128)} %param.31) | copy-start | bytes 7077892
  172.8 212.3 %all-reduce.9.cloned.1.call-start = ((), (), s32[]{:S(2)}) async-start(), calls=%async_computation.1 | async-start | bytes 9437184 | tf_op jit(solution)/shard_map/psum | solution.py:129
  273.5 3.1 copy-start.44
  273.7 6.6 slice-start.3
  273.7 6.7 slice-start.5
  276.6 3.7 copy-start.35
  276.6 3.7 copy-start.53
  276.6 3.7 slice-start.4
  276.6 3.7 slice-start.6
  280.3 4.8 copy-start.3
  280.4 6.1 copy-start.33
  290.7 6.8 copy-start.20
  290.7 6.8 copy-start.29
  290.7 6.8 copy-start.43
  290.7 396.0 %all-reduce.13.cloned.1.call-start = ((), (), s32[]{:S(2)}) async-start(), calls=%async_computation.6 | async-start | bytes 15728640 | tf_op jit(solution)/shard_map/psum | solution.py:190
  290.8 6.7 copy-start.58
  303.5 88.9 %copy-start.26 = (f32[1536]{0:T(1024)S(1)}, f32[1536]{0:T(1024)}, u32[]{:S(2)}) copy-start(f32[1536]{0:T(1024)} %copy-done.25) | copy-start | bytes 18436
  396.0 2.4 copy-start.2
  399.5 6.4 copy-start.8
  399.6 12.1 %slice-start = ((s8[9437184]{0:T(1024)(128)(4,1)}), s8[4194304]{0:T(1024)(128)(4,1)S(1)}, s32[]{:S(2)}) async-start(s8[9437184]{0:T(1024)(128)(4,1)} %bitcast.159), calls=%async_computation.7 | async-start | bytes 8388608
  399.6 12.1 %slice-start.1 = ((s8[9437184]{0:T(1024)(128)(4,1)}), s8[4194304]{0:T(1024)(128)(4,1)S(1)}, s32[]{:S(2)}) async-start(s8[9437184]{0:T(1024)(128)(4,1)} %bitcast.159), calls=%async_computation.8 | async-start | bytes 8388608
  406.0 5.7 slice-start.2
  411.7 2.4 copy-start.5
  411.7 2.4 copy-start.24
  429.2 352.9 %all-reduce.11.cloned.1.call-start = ((), (), s32[]{:S(2)}) async-start(), calls=%async_computation.2 | async-start | bytes 9437184 | tf_op jit(solution)/shard_map/psum | solution.py:164
  435.0 263.1 %copy-start.40 = (f32[768]{0:T(1024)S(1)}, f32[768]{0:T(1024)}, u32[]{:S(2)}) copy-start(f32[768]{0:T(1024)} %get-tuple-element.66) | copy-start | bytes 9220
  435.0 263.2 %copy-start.41 = (f32[768]{0:T(1024)S(1)}, f32[768]{0:T(1024)}, u32[]{:S(2)}) copy-start(f32[768]{0:T(1024)} %get-tuple-element.69) | copy-start | bytes 9220
  435.0 263.2 %copy-start.6 = (bf16[1536,768]{0,1:T(8,128)(2,1)S(1)}, bf16[1536,768]{0,1:T(8,128)(2,1)}, u32[]{:S(2)}) copy-start(bf16[1536,768]{0,1:T(8,128)(2,1)} %get-tuple-element.97) | copy-start | bytes 7077892
  435.0 443.9 %all-gather.4.cloned.1.call-start = ((), (), s32[]{:S(2)}) async-start(), calls=%async_computation.3 | async-start | bytes 2654208 | tf_op jit(solution)/shard_map/all_gather | solution.py:215
  689.0 205.3 %all-gather.6.cloned.1.call-start = ((), (), s32[]{:S(2)}) async-start(), calls=%async_computation.4 | async-start | bytes 2654208 | tf_op jit(solution)/shard_map/all_gather | solution.py:217
  691.3 256.3 %all-gather.8.cloned.1.call-start = ((), (), s32[]{:S(2)}) async-start(), calls=%async_computation.5 | async-start | bytes 2654208 | tf_op jit(solution)/shard_map/all_gather | solution.py:218
  696.2 4.4 copy-start.51
  696.2 4.7 copy-start.45
  696.2 4.7 copy-start.47
  696.2 4.7 copy-start.46
  696.2 4.8 copy-start.49
  696.2 4.8 copy-start.50
  701.4 128.8 %copy-start.22 = (f32[6,768]{1,0:T(8,128)S(1)}, f32[6,768]{1,0:T(8,128)}, u32[]{:S(2)}) copy-start(f32[6,768]{1,0:T(8,128)} %param.33) | copy-start | bytes 55300
  831.5 6.2 copy-start.38
  831.5 6.2 copy-start.48
  831.5 7.4 copy-start.30
  831.5 7.4 copy-start.31
  831.5 7.4 copy-start.39
  831.5 8.7 copy-start.18
  831.6 44.7 %copy-start.12 = (f32[1,96,3,192]{3,1,2,0:T(8,128)S(1)}, f32[1,96,3,192]{3,1,2,0:T(8,128)}, u32[]{:S(2)}) copy-start(f32[1,96,3,192]{3,1,2,0:T(8,128)} %get-tuple-element.110) | copy-start | bytes 663556
  837.7 39.4 %copy-start.14 = (f32[1,96,768]{2,1,0:T(8,128)S(1)}, f32[1,96,768]{2,1,0:T(8,128)}, u32[]{:S(2)}) copy-start(f32[1,96,768]{2,1,0:T(8,128)} %get-tuple-element.103) | copy-start | bytes 884740
  837.7 39.4 %copy-start.15 = (f32[1,96,768]{2,1,0:T(8,128)S(1)}, f32[1,96,768]{2,1,0:T(8,128)}, u32[]{:S(2)}) copy-start(f32[1,96,768]{2,1,0:T(8,128)} %get-tuple-element.104) | copy-start | bytes 884740
  837.7 40.3 %copy-start.13 = (f32[1,96,768]{2,1,0:T(8,128)S(1)}, f32[1,96,768]{2,1,0:T(8,128)}, u32[]{:S(2)}) copy-start(f32[1,96,768]{2,1,0:T(8,128)} %get-tuple-element.107) | copy-start | bytes 884740
  947.6 3.4 copy-start.11
  (11 other events, 12.5 us)
Sparse Core Ops, SparseCore 0:
  172.9 95.4 all-reduce.6
  290.8 94.1 all-reduce.8
  429.3 257.4 all-reduce.12
  689.0 93.0 all-reduce.10
  784.7 52.6 all-gather.3
  840.0 54.2 all-gather.5
  896.5 51.0 all-gather.7
